TPU v7x, 256 devices: a whole 4x4x8 slice. The times are simulated.
256 devices in a mesh: member: 16 (over x, z_hi), cell: 16 (over y, z_lo, core).
Axes of the slice: x: 4, y: 4, z: 8 (z_hi: 4, z_lo: 2; z = z_hi * 2 + z_lo), core: 2. Of those that a mesh axis runs over, the one named last changes fastest.
Arguments:
- latent: bfloat16 [16, 24576, 1024], P('member', 'cell'), may hold values from -6 to 6
- w_in: bfloat16 [1024, 1024], replicated, may hold values from -0.1875 to 0.1875
- w_out: bfloat16 [1024, 96], replicated, may hold values from -0.1875 to 0.1875
- target: bfloat16 [96, 24576], P(None, 'cell'), may hold values from -6 to 6
- cell_mask: int32 [24576], P('cell'), may hold values 0 or 1
Outputs:
- grad_w_in: float32 [1024, 1024], P(('member', 'cell'))
- grad_w_out: float32 [1024, 96], P(('member', 'cell'))
All inputs are finite; a program needn't handle non-finite values. No bound on the sum of `cell_mask` on one device may be relied on, other than what follows from the above.
Results may differ from a plain program's by a relative error of at most 0.0055.
Values may be sent and summed in bfloat16 or wider, within the bound.
No kernel may reach another device: no remote copies, remote signals or barrier semaphores. Data moves between devices by JAX's collectives and lax.ppermute only.
A program may use at most 64 MiB of HBM per device.

v0:
```python
import jax
import jax.numpy as jnp
from jax import lax
from jax.sharding import PartitionSpec as P


def in_blocks(x, dim, peers):
    before, after = (x.shape[:dim], x.shape[dim + 1 :])
    return jnp.moveaxis(x.reshape(*before, peers, -1, *after), dim, 0)


def summed_on_arrival(x, axis, dim):
    peers = lax.axis_size(axis)
    tiles = lax.all_to_all(in_blocks(x, dim, peers), axis, 0, 0, tiled=True)
    return jnp.sum(tiles.astype(jnp.float32), axis=0)


def sent_and_summed(x, axis, dim):
    peers = lax.axis_size(axis)
    tiles = lax.all_to_all(in_blocks(x, dim, peers), axis, 0, 0, tiled=True)
    return jnp.sum(tiles, axis=0)


def kernel_fn(diff):
    return diff / jnp.sqrt(1.0 + diff * diff)


def silu_slope(pre):
    gate = jax.nn.sigmoid(pre)
    return gate * (1.0 + pre * (1.0 - gate))


def per_device(latent, w_in, w_out, target, cell_mask):
    members = lax.axis_size("member")
    cell_count = lax.axis_size("cell")
    own_latent = latent[0]
    cells_here = own_latent.shape[0]
    scale = 1.0 / jnp.sqrt(jnp.float32(cells_here * cell_count))
    pre = jnp.dot(own_latent, w_in, preferred_element_type=jnp.float32)
    hidden = jax.nn.silu(pre).astype(jnp.bfloat16)
    fields = lax.dot_general(
        w_out, hidden, (((0,), (1,)), ((), ())), preferred_element_type=jnp.float32
    ).astype(jnp.bfloat16)
    wide = fields.astype(jnp.float32)
    values = lax.all_to_all(fields[None], "member", split_axis=2, concat_axis=0, tiled=True).astype(
        jnp.float32
    )
    sums = jnp.sum(kernel_fn(values[:, None] - values[None, :]), axis=1)
    pair = lax.all_to_all(sums, "member", split_axis=0, concat_axis=2, tiled=True)[0]
    weight = cell_mask.astype(jnp.float32) * scale / members
    own_term = kernel_fn(wide - target.astype(jnp.float32))
    grad_fields = (weight[None] * (own_term - pair / members)).astype(jnp.bfloat16)
    back = lax.dot_general(
        grad_fields, w_out, (((0,), (1,)), ((), ())), preferred_element_type=jnp.float32
    )
    grad_pre = (back * silu_slope(pre)).astype(jnp.bfloat16)
    width = w_in.shape[1]
    grad_in = lax.dot_general(
        own_latent, grad_pre, (((0,), (0,)), ((), ())), preferred_element_type=jnp.float32
    )
    grad_out = lax.dot_general(
        hidden, grad_fields, (((0,), (1,)), ((), ())), preferred_element_type=jnp.float32
    )
    partial_rows = summed_on_arrival(
        jnp.concatenate([grad_in, grad_out], axis=1).astype(jnp.bfloat16), "member", 0
    )
    owned = sent_and_summed(partial_rows, "cell", 0)
    return (owned[:, :width], owned[:, width:])


def solution(mesh):
    in_specs = (P("member", "cell", None), P(), P(), P(None, "cell"), P("cell"))
    out_specs = (P(("member", "cell"), None), P(("member", "cell"), None))
    return jax.shard_map(
        per_device, mesh=mesh, in_specs=in_specs, out_specs=out_specs, check_vma=False
    )
```

profile of v0, /device:TPU:1, one launch (start us, length us, event | category | flops | bytes accessed | tf_op | source)
XLA Modules:
  0.0 188.8 jit_solution(4087096693529205506)
XLA Ops:
  0.6 0.0 copy-start
  0.6 0.0 copy-start.3
  0.7 1.9 copy-done
  2.5 7.5 %multiply_convert_fusion.1 = (bf16[1536,1024]{1,0:T(8,128)(2,1)S(1)}, f32[1536,1024]{1,0:T(8,128)}) fusion(bf16[1024,1024]{1,0:T(8,128)(2,1)} %param.6, bf16[1,1536,1024]{2,1,0:T(8,128)(2,1)S(1)} %copy-done), kind=kOutput, calls=%fused_computation.6 | convolution fusion | flops 3229089792 | bytes 14680064 | tf_op jit(solution)/shard_map/dot_general | solution.py:39
  10.0 0.0 copy-start.1
  10.0 1.7 copy-done.1
  11.7 0.0 copy-done.3
  11.7 1.1 convolution_convert_fusion
  12.8 1.8 copy.23
  14.6 0.5 broadcast.13
  15.1 10.5 %reduce = bf16[1536,96]{1,0:T(8,128)(2,1)} reduce(bf16[1536,1,96]{2,1,0:T(2,128)(2,1)} %bitcast.40, bf16[]{:T(256)} %broadcast.13), dimensions={1}, to_apply=%bitcast.26.reduce_sub_computation | reduce | bytes 589826
  25.7 2.3 %reshape.32 = bf16[16,2,4608]{2,1,0:T(2,128)(2,1)} reshape(bf16[1536,96]{1,0:T(8,128)(2,1)} %reduce) | data formatting | bytes 589824
  27.9 24.5 %all_to_all.28 = bf16[16,2,4608]{2,1,0:T(2,128)(2,1)} all-to-all(bf16[16,2,4608]{2,1,0:T(2,128)(2,1)} %reshape.32), channel_id=1, replica_groups=mesh['member'=16,'cell'=16] {'member'}, dimensions={0} | all-to-all | bytes 589824 | tf_op jit(solution)/shard_map/all_to_all | solution.py:45
  52.5 4.0 %reshape.33 = bf16[1536,1,96]{2,1,0:T(2,128)(2,1)} reshape(bf16[16,2,4608]{2,1,0:T(2,128)(2,1)} %all_to_all.28) | data formatting | bytes 589824
  56.5 0.0 copy-start.4
  56.5 2.6 %bitcast_convert_fusion = f32[1,96,1536]{1,0,2:T(1,128)} fusion(bf16[1536,1,96]{2,1,0:T(2,128)(2,1)} %reshape.33), kind=kLoop, calls=%fused_computation.21 | loop fusion | flops 147456 | bytes 884736 | tf_op jit(solution)/shard_map/sub | solution.py:48
  59.1 2.3 %copy.24 = f32[16,96,96]{2,1,0:T(8,128)} copy(f32[16,96,96]{1,2,0:T(8,128)} %bitcast.39) | data formatting | bytes 1179648 | tf_op jit(solution)/shard_map/sub | solution.py:48
  61.4 5.2 %fusion.2 = f32[16,96,96]{2,1,0:T(8,128)} fusion(f32[16,96,96]{2,1,0:T(8,128)} %copy.24), kind=kLoop, calls=%fused_computation.4 | loop fusion | flops 11649024 | bytes 1179648 | tf_op jit(solution)/shard_map/reduce_sum | solution.py:48
  66.6 4.5 %all-to-all-start.1 = ((f32[16,96,96]{2,1,0:T(8,128)}), f32[16,96,96]{2,1,0:T(8,128)}, u32[]{:S(2)}, u32[]{:S(2)}) async-start(f32[16,96,96]{2,1,0:T(8,128)} %fusion.2), calls=%async_computation.1 | async-start | bytes 1572864 | tf_op jit(solution)/shard_map/all_to_all | solution.py:49
  71.1 0.0 copy-done.4
  71.1 19.8 %all-to-all-done.1 = f32[16,96,96]{2,1,0:T(8,128)} async-done(((f32[16,96,96]{2,1,0:T(8,128)}), f32[16,96,96]{2,1,0:T(8,128)}, u32[]{:S(2)}, u32[]{:S(2)}) %all-to-all-start.1) | async-done | bytes 589856 | tf_op jit(solution)/shard_map/all_to_all | solution.py:49
  90.9 1.2 multiply_bitcast_fusion
  92.1 1.3 copy.26
  93.5 2.3 %div.38 = f32[96,1536]{1,0:T(8,128)} reshape(f32[1,96,16,96]{3,2,1,0:T(8,128)} %copy.26) | data formatting | bytes 1179648 | tf_op jit(solution)/shard_map/div | solution.py:52
  95.7 1.3 multiply_convert_fusion.2
  97.1 0.0 copy-start.2
  97.1 0.7 copy-done.2
  97.8 3.2 %convolution_convert_fusion.1 = bf16[1024,96]{0,1:T(8,128)(2,1)} fusion(bf16[96,1536]{1,0:T(8,128)(2,1)S(1)} %multiply_convert_fusion.2, bf16[1536,1024]{1,0:T(8,128)(2,1)} %copy-done.1), kind=kOutput, calls=%fused_computation.16 | convolution fusion | flops 302088192 | bytes 3637248 | tf_op jit(solution)/shard_map/dot_general | solution.py:61
  101.0 1.1 copy.27
  102.1 7.8 %fusion.7 = bf16[1024,1024]{0,1:T(8,128)(2,1)} fusion(bf16[1,1536,1024]{2,1,0:T(8,128)(2,1)S(1)} %copy-done, f32[1536,1024]{1,0:T(8,128)} %get-tuple-element.3, bf16[96,1536]{1,0:T(8,128)(2,1)} %copy-done.2, bf16[1024,96]{0,1:T(8,128)(2,1)} %param.7), kind=kOutput, calls=%fused_computation.15 | convolution fusion | flops 3538419712 | bytes 12025856 | tf_op jit(solution)/shard_map/dot_general | solution.py:58
  109.9 1.8 pad_maximum_fusion
  111.7 45.2 %all_to_all.29 = bf16[16,64,1120]{2,1,0:T(8,128)(2,1)S(1)} all-to-all(bf16[16,64,1120]{2,1,0:T(8,128)(2,1)S(1)} %pad_maximum_fusion), channel_id=1, replica_groups=mesh['member'=16,'cell'=16] {'member'}, dimensions={0} | all-to-all | bytes 4587520 | tf_op jit(solution)/shard_map/all_to_all | solution.py:14
  156.9 0.3 convert_reduce_fusion
  157.2 0.8 reshape.29
  158.0 29.6 %all_to_all.30 = f32[16,4,1120]{2,1,0:T(4,128)S(1)} all-to-all(f32[16,4,1120]{2,1,0:T(4,128)} %reshape.29), channel_id=1, replica_groups=mesh['member'=16,'cell'=16] {'cell'}, dimensions={0} | all-to-all | bytes 573440 | tf_op jit(solution)/shard_map/all_to_all | solution.py:20
  187.6 0.1 reduce_sum.29
  187.7 0.6 slice.8
  188.3 0.6 slice.9
  (1 shorter events, 0.0 us)
Async XLA Ops:
  0.6 1.9 %copy-start = (bf16[1,1536,1024]{2,1,0:T(8,128)(2,1)S(1)}, bf16[1,1536,1024]{2,1,0:T(8,128)(2,1)}, u32[]{:S(2)}) copy-start(bf16[1,1536,1024]{2,1,0:T(8,128)(2,1)} %param.5) | copy-start | bytes 9437188
  0.6 11.1 %copy-start.3 = (bf16[1024,96]{0,1:T(8,128)(2,1)S(1)}, bf16[1024,96]{0,1:T(8,128)(2,1)}, u32[]{:S(2)}) copy-start(bf16[1024,96]{0,1:T(8,128)(2,1)} %param.7) | copy-start | bytes 589828
  10.0 1.7 copy-start.1
  56.5 14.6 %copy-start.4 = (s32[1536]{0:T(1024)S(1)}, s32[1536]{0:T(1024)}, u32[]{:S(2)}) copy-start(s32[1536]{0:T(1024)} %param.9) | copy-start | bytes 18436
  66.6 24.3 %all-to-all-start.1 = ((f32[16,96,96]{2,1,0:T(8,128)}), f32[16,96,96]{2,1,0:T(8,128)}, u32[]{:S(2)}, u32[]{:S(2)}) async-start(f32[16,96,96]{2,1,0:T(8,128)} %fusion.2), calls=%async_computation.1 | async-start | bytes 1572864 | tf_op jit(solution)/shard_map/all_to_all | solution.py:49
  97.1 0.7 copy-start.2
where the time goes:
time: 190 us; the launch traced here: 189 us
  blocking collectives  99.3 us (52%)
  other arithmetic  23.1 us (12%)
  local copies, waits for them, and re-layouts  21.8 us (11%)
  waiting for transfers between devices  19.8 us (10%)
  matrix products  19.6 us (10%)
  starting transfers between devices  4.46 us (2%)
    all_to_all x1, blocking collectives, summed_on_arrival(): tiles = lax.all_to_all(in_blocks(x, dim, peers), axis, 0, 0, tiled=True)  45.2 us
    all_to_all x1, blocking collectives, sent_and_summed(): tiles = lax.all_to_all(in_blocks(x, dim, peers), axis, 0, 0, tiled=True)  29.6 us
    all_to_all x1, blocking collectives, per_device(): lax.all_to_all(fields[None], 'member', split_axis=2, concat_axis=0, tiled...  24.5 us
    all_to_all x1, waiting for transfers between devices, per_device(): lax.all_to_all(sums, 'member', split_axis=0, concat_axis=2, tiled=True)[0]  19.8 us
    unnamed x13, local copies, waits for them, and re-layouts  11.1 us
    unnamed x1, other arithmetic  10.5 us
    dot_general x1, matrix products, per_device(): lax.dot_general(own_latent, grad_pre, (((0,), (0,)), ((), ())), preferred...  7.77 us
    dot_general x1, matrix products, per_device(): pre = jnp.dot(own_latent, w_in, preferred_element_type=jnp.float32)  7.5 us
  transfers between devices with their start and end apart: 1, of which 1 were waited for; matrix products, arithmetic and copies ran while one was open for 0% of the time, Pallas kernels for 0%

commit v1 on v0

--- a/solution.py
+++ b/solution.py
@@ -42,9 +42,12 @@
         w_out, hidden, (((0,), (1,)), ((), ())), preferred_element_type=jnp.float32
     ).astype(jnp.bfloat16)
     wide = fields.astype(jnp.float32)
-    values = lax.all_to_all(fields[None], "member", split_axis=2, concat_axis=0, tiled=True).astype(
-        jnp.float32
-    )
+    values = jnp.concatenate(
+        lax.all_to_all(
+            jnp.stack(jnp.split(fields[None], lax.axis_size("member"), axis=2)), "member", 0, 0
+        ),
+        axis=0,
+    ).astype(jnp.float32)
     sums = jnp.sum(kernel_fn(values[:, None] - values[None, :]), axis=1)
     pair = lax.all_to_all(sums, "member", split_axis=0, concat_axis=2, tiled=True)[0]
     weight = cell_mask.astype(jnp.float32) * scale / members

time: 190 us -> 167 us (0.88)
  other arithmetic: 23.1 us -> 8.6 us
  local copies, waits for them, and re-layouts: 21.8 us -> 12.1 us
    unnamed x1 -> x0, other arithmetic: 10.5 us -> none
    unnamed x13 -> x25, local copies, waits for them, and re-layouts: 11.1 us -> 5.29 us
    sub x1, other arithmetic: 2.6 us -> 0.07 us  [per_device(): sums = jnp.sum(kernel_fn(values[:, None] - values[None, :]), axis=1)]
    sub x1 -> x0, local copies, waits for them, and re-layouts: 2.29 us -> none  [per_device(): sums = jnp.sum(kernel_fn(values[:, None] - values[None, :]), axis=1)]
where the time goes in v1:
time: 167 us; the launch traced here: 166 us
  blocking collectives  101 us (60%)
  waiting for transfers between devices  20.6 us (12%)
  matrix products  19.5 us (12%)
  local copies, waits for them, and re-layouts  12.1 us (7%)
  other arithmetic  8.6 us (5%)
  starting transfers between devices  4.28 us (3%)
    all_to_all x1, blocking collectives, summed_on_arrival(): tiles = lax.all_to_all(in_blocks(x, dim, peers), axis, 0, 0, tiled=True)  44.6 us
    all_to_all x1, blocking collectives, sent_and_summed(): tiles = lax.all_to_all(in_blocks(x, dim, peers), axis, 0, 0, tiled=True)  29.9 us
    all_to_all x1, blocking collectives, per_device(): lax.all_to_all(jnp.stack(jnp.split(fields[None], lax.axis_size('member'),...  26 us
    all_to_all x1, waiting for transfers between devices, per_device(): lax.all_to_all(sums, 'member', split_axis=0, concat_axis=2, tiled=True)[0]  20.6 us
    dot_general x1, matrix products, per_device(): lax.dot_general(own_latent, grad_pre, (((0,), (0,)), ((), ())), preferred...  7.72 us
    dot_general x1, matrix products, per_device(): pre = jnp.dot(own_latent, w_in, preferred_element_type=jnp.float32)  7.51 us
    unnamed x25, local copies, waits for them, and re-layouts  5.29 us
    all_to_all x1, starting transfers between devices, per_device(): lax.all_to_all(sums, 'member', split_axis=0, concat_axis=2, tiled=True)[0]  4.28 us
  transfers between devices with their start and end apart: 1, of which 1 were waited for; matrix products, arithmetic and copies ran while one was open for 0% of the time, Pallas kernels for 0%

profile of v1, /device:TPU:1, one launch (start us, length us, event | category | flops | bytes accessed | tf_op | source)
XLA Modules:
  0.0 166.4 jit_solution(9355427910668691714)
XLA Ops:
  0.6 0.0 copy-start
  0.6 0.0 copy-start.3
  0.7 1.9 %copy-done = bf16[1,1536,1024]{2,1,0:T(8,128)(2,1)S(1)} copy-done((bf16[1,1536,1024]{2,1,0:T(8,128)(2,1)S(1)}, bf16[1,1536,1024]{2,1,0:T(8,128)(2,1)}, u32[]{:S(2)}) %copy-start) | copy-done | bytes 3145752
  2.5 7.5 %multiply_convert_fusion.1 = (bf16[1536,1024]{1,0:T(8,128)(2,1)S(1)}, f32[1536,1024]{1,0:T(8,128)}) fusion(bf16[1024,1024]{1,0:T(8,128)(2,1)} %param.6, bf16[1,1536,1024]{2,1,0:T(8,128)(2,1)S(1)} %copy-done), kind=kOutput, calls=%fused_computation.6 | convolution fusion | flops 3229089792 | bytes 14680064 | tf_op jit(solution)/shard_map/dot_general | solution.py:39
  10.0 0.0 copy-start.1
  10.0 1.7 %copy-done.1 = bf16[1536,1024]{1,0:T(8,128)(2,1)} copy-done((bf16[1536,1024]{1,0:T(8,128)(2,1)}, bf16[1536,1024]{1,0:T(8,128)(2,1)S(1)}, u32[]{:S(2)}) %copy-start.1) | copy-done | bytes 3145752
  11.7 0.0 copy-done.3
  11.7 1.1 convolution_convert_fusion
  12.8 0.0 copy-start.4
  12.9 0.1 constant_dynamic-update-slice_fusion.14
  12.9 0.1 constant_dynamic-update-slice_fusion.13
  13.0 0.1 constant_dynamic-update-slice_fusion.12
  13.1 0.1 constant_dynamic-update-slice_fusion.10
  13.2 0.1 constant_dynamic-update-slice_fusion.9
  13.3 0.1 constant_dynamic-update-slice_fusion.8
  13.4 0.1 constant_dynamic-update-slice_fusion.6
  13.5 0.1 constant_dynamic-update-slice_fusion.5
  13.6 0.1 constant_dynamic-update-slice_fusion.4
  13.7 0.1 constant_dynamic-update-slice_fusion.2
  13.8 0.1 constant_dynamic-update-slice_fusion.1
  13.9 0.1 constant_dynamic-update-slice_fusion
  14.0 26.0 %all_to_all.24 = bf16[16,1,96,96]{3,2,1,0:T(8,128)(2,1)S(1)} all-to-all(bf16[16,1,96,96]{3,2,1,0:T(8,128)(2,1)S(1)} %constant_dynamic-update-slice_fusion), channel_id=1, replica_groups=mesh['member'=16,'cell'=16] {'member'}, dimensions={0} | all-to-all | bytes 589824 | tf_op jit(solution)/shard_map/all_to_all | solution.py:46
  40.0 0.1 bitcast_convert_fusion
  40.1 3.8 %fusion.2 = f32[16,96,96]{2,1,0:T(8,128)} fusion(f32[16,96,96]{2,1,0:T(8,128)S(1)} %bitcast_convert_fusion), kind=kLoop, calls=%fused_computation.4 | loop fusion | flops 11649024 | bytes 1179648 | tf_op jit(solution)/shard_map/reduce_sum | solution.py:51
  43.9 4.3 %all-to-all-start.1 = ((f32[16,96,96]{2,1,0:T(8,128)}), f32[16,96,96]{2,1,0:T(8,128)}, u32[]{:S(2)}, u32[]{:S(2)}) async-start(f32[16,96,96]{2,1,0:T(8,128)} %fusion.2), calls=%async_computation.1 | async-start | bytes 1572864 | tf_op jit(solution)/shard_map/all_to_all | solution.py:52
  48.1 0.0 copy-done.4
  48.2 20.6 %all-to-all-done.1 = f32[16,96,96]{2,1,0:T(8,128)} async-done(((f32[16,96,96]{2,1,0:T(8,128)}), f32[16,96,96]{2,1,0:T(8,128)}, u32[]{:S(2)}, u32[]{:S(2)}) %all-to-all-start.1) | async-done | bytes 589856 | tf_op jit(solution)/shard_map/all_to_all | solution.py:52
  68.7 1.2 multiply_bitcast_fusion
  69.9 1.3 copy.13
  71.3 2.3 %div.38 = f32[96,1536]{1,0:T(8,128)} reshape(f32[1,96,16,96]{3,2,1,0:T(8,128)} %copy.13) | data formatting | bytes 1179648 | tf_op jit(solution)/shard_map/div | solution.py:55
  73.6 1.3 multiply_convert_fusion.2
  74.9 0.0 copy-start.2
  74.9 0.7 copy-done.2
  75.6 3.2 %convolution_convert_fusion.1 = bf16[1024,96]{0,1:T(8,128)(2,1)} fusion(bf16[96,1536]{1,0:T(8,128)(2,1)S(1)} %multiply_convert_fusion.2, bf16[1536,1024]{1,0:T(8,128)(2,1)} %copy-done.1), kind=kOutput, calls=%fused_computation.16 | convolution fusion | flops 302088192 | bytes 3637248 | tf_op jit(solution)/shard_map/dot_general | solution.py:64
  78.8 1.1 copy.14
  79.9 7.7 %fusion.7 = bf16[1024,1024]{0,1:T(8,128)(2,1)} fusion(bf16[1,1536,1024]{2,1,0:T(8,128)(2,1)S(1)} %copy-done, f32[1536,1024]{1,0:T(8,128)} %get-tuple-element.3, bf16[96,1536]{1,0:T(8,128)(2,1)} %copy-done.2, bf16[1024,96]{0,1:T(8,128)(2,1)} %param.7), kind=kOutput, calls=%fused_computation.15 | convolution fusion | flops 3538419712 | bytes 12025856 | tf_op jit(solution)/shard_map/dot_general | solution.py:61
  87.6 1.8 %pad_maximum_fusion = bf16[16,64,1120]{2,1,0:T(8,128)(2,1)S(1)} fusion(bf16[16,64,96]{2,1,0:T(8,128)(2,1)S(1)} %bitcast.114, bf16[16,64,1024]{2,1,0:T(8,128)(2,1)} %bitcast.113), kind=kLoop, calls=%fused_computation.13 | loop fusion | flops 4587520 | bytes 4587520 | tf_op jit(solution)/shard_map/concatenate | solution.py:68
  89.5 44.6 %all_to_all.25 = bf16[16,64,1120]{2,1,0:T(8,128)(2,1)S(1)} all-to-all(bf16[16,64,1120]{2,1,0:T(8,128)(2,1)S(1)} %pad_maximum_fusion), channel_id=1, replica_groups=mesh['member'=16,'cell'=16] {'member'}, dimensions={0} | all-to-all | bytes 4587520 | tf_op jit(solution)/shard_map/all_to_all | solution.py:14
  134.1 0.3 convert_reduce_fusion
  134.5 0.8 reshape.26
  135.3 29.9 %all_to_all.26 = f32[16,4,1120]{2,1,0:T(4,128)S(1)} all-to-all(f32[16,4,1120]{2,1,0:T(4,128)} %reshape.26), channel_id=1, replica_groups=mesh['member'=16,'cell'=16] {'cell'}, dimensions={0} | all-to-all | bytes 573440 | tf_op jit(solution)/shard_map/all_to_all | solution.py:20
  165.2 0.1 reduce_sum.29
  165.2 0.6 slice.8
  165.8 0.6 slice.9
  (5 shorter events, 0.0 us)
Async XLA Ops:
  0.6 1.9 %copy-start = (bf16[1,1536,1024]{2,1,0:T(8,128)(2,1)S(1)}, bf16[1,1536,1024]{2,1,0:T(8,128)(2,1)}, u32[]{:S(2)}) copy-start(bf16[1,1536,1024]{2,1,0:T(8,128)(2,1)} %param.5) | copy-start | bytes 9437188
  0.6 11.1 %copy-start.3 = (bf16[1024,96]{0,1:T(8,128)(2,1)S(1)}, bf16[1024,96]{0,1:T(8,128)(2,1)}, u32[]{:S(2)}) copy-start(bf16[1024,96]{0,1:T(8,128)(2,1)} %param.7) | copy-start | bytes 589828
  10.0 1.7 %copy-start.1 = (bf16[1536,1024]{1,0:T(8,128)(2,1)}, bf16[1536,1024]{1,0:T(8,128)(2,1)S(1)}, u32[]{:S(2)}) copy-start(bf16[1536,1024]{1,0:T(8,128)(2,1)S(1)} %get-tuple-element.2) | copy-start | bytes 9437188
  12.8 35.3 %copy-start.4 = (s32[1536]{0:T(1024)S(1)}, s32[1536]{0:T(1024)}, u32[]{:S(2)}) copy-start(s32[1536]{0:T(1024)} %param.9) | copy-start | bytes 18436
  43.9 24.9 %all-to-all-start.1 = ((f32[16,96,96]{2,1,0:T(8,128)}), f32[16,96,96]{2,1,0:T(8,128)}, u32[]{:S(2)}, u32[]{:S(2)}) async-start(f32[16,96,96]{2,1,0:T(8,128)} %fusion.2), calls=%async_computation.1 | async-start | bytes 1572864 | tf_op jit(solution)/shard_map/all_to_all | solution.py:52
  74.9 0.7 copy-start.2
